TPU v7x, 256 devices: a whole 4x4x8 slice. The times are simulated.
256 devices in a mesh: outer: 8 (over z), inner: 32 (over x, y, core).
Axes of the slice: x: 4, y: 4, z: 8, core: 2. Of those that a mesh axis runs over, the one named last changes fastest.
Arguments:
- b_leaf: float32 [65536, 64], P(('outer', 'inner')), may hold values from -6 to 6
- b_sep: float32 [2048, 64], P(('outer', 'inner')), may hold values from -6 to 6
- b_root: float32 [2048, 64], P(('outer', 'inner')), may hold values from -6 to 6
- leaf_linv: float32 [65536, 256], P(('outer', 'inner')), as said below
- leaf_uinv: float32 [65536, 256], P(('outer', 'inner')), as said below
- leaf_lower: float32 [65536, 256], P(('outer', 'inner')), as said below
- leaf_upper: float32 [65536, 256], P(('outer', 'inner')), as said below
- sep_rows: int32 [256, 256], P(('outer', 'inner')), may hold values from 0 to 255, as said below
- sep_linv: float32 [2048, 256], P(('outer', 'inner')), as said below
- sep_uinv: float32 [2048, 256], P(('outer', 'inner')), as said below
- sep_lower: float32 [2048, 2048], P(None, ('outer', 'inner')), as said below
- sep_upper: float32 [2048, 2048], P(('outer', 'inner')), as said below
- root_linv: float32 [2048, 2048], P(('outer', 'inner')), as said below
- root_uinv: float32 [2048, 2048], P(('outer', 'inner')), as said below
- basis_leaf: float32 [65536, 512], P(('outer', 'inner')), as said below
- basis_sep: float32 [2048, 512], P(('outer', 'inner')), as said below
- basis_root: float32 [2048, 512], P(('outer', 'inner')), as said below
- g_blocks: float32 [262144, 128], P(('outer', 'inner')), may hold values from -0.25 to 0.25
- c_blocks: float32 [262144, 128], P(('outer', 'inner')), may hold values from -0.25 to 0.25
- block_cols: int32 [512, 4], P(('outer', 'inner')), may hold values from 0 to 1
Outputs:
- v_leaf: float32 [65536, 64], P(('outer', 'inner'))
- v_sep: float32 [2048, 64], P(('outer', 'inner'))
- v_root: float32 [2048, 64], P(('outer', 'inner'))
- coefficients: float32 [512, 64], replicated
- reduced_g: float32 [64, 64], replicated
- reduced_c: float32 [64, 64], replicated
Inputs may be any that keep to these rules, and one draw needn't show every extreme that they name: `sep_rows`: each row holds 256 distinct numbers; every row names 0 and 255. `leaf_linv`: lower triangular in each diagonal block of the stack, nonzero diagonal. `leaf_uinv`: upper triangular in each diagonal block of the stack, nonzero diagonal. `sep_linv`: lower triangular in each block of 256 rows, nonzero diagonal. `sep_uinv`: upper triangular in each block of 256 rows, nonzero diagonal. `root_linv`: lower triangular, nonzero diagonal. `root_uinv`: upper triangular, nonzero diagonal. `leaf_lower`: entries of order one over the square root of 256. `leaf_upper`: entries of order one over the square root of 256. `sep_lower`: entries of order one over the square root of the number of its columns. `sep_upper`: entries of order one over the square root of 2048. basis_leaf, basis_sep and basis_root stacked by rows form Q with Q^T Q = 69632 I up to float32 rounding. `basis_sep`: part of the stacked Q described with basis_leaf. `basis_root`: part of the stacked Q described with basis_leaf.
All inputs are finite; a program needn't handle non-finite values.
Results may differ from a plain program's by a relative error of at most 0.0003.
Values sent between devices are 32-bit elements; how exact they have to be, the bound alone decides.
A program may use at most 64 MiB of HBM per device.

v0:
```python
import jax
import jax.numpy as jnp
from jax import lax
from jax.sharding import PartitionSpec as P


def matmul_exact(left, right):
    return jnp.dot(left, right, precision=lax.Precision.HIGHEST, preferred_element_type=jnp.float32)


def contract_rows(left, right):
    return lax.dot_general(
        left,
        right,
        (((0,), (0,)), ((), ())),
        precision=lax.Precision.HIGHEST,
        preferred_element_type=jnp.float32,
    )


def shards(
    b_leaf,
    b_sep,
    b_root,
    leaf_linv,
    leaf_uinv,
    leaf_lower,
    leaf_upper,
    sep_rows,
    sep_linv,
    sep_uinv,
    sep_lower,
    sep_upper,
    root_linv,
    root_uinv,
    basis_leaf,
    basis_sep,
    basis_root,
    g_blocks,
    c_blocks,
    block_cols,
):
    ports = b_leaf.shape[1]
    sep_local = b_sep.shape[0]
    root_local = b_root.shape[0]
    sep_width = sep_linv.shape[1]
    selector = (sep_rows[0][:, None] == jnp.arange(sep_width, dtype=jnp.int32)[None, :]).astype(
        jnp.float32
    )
    y_leaf = matmul_exact(leaf_linv, b_leaf)
    contrib = matmul_exact(leaf_lower, y_leaf)
    t_sep = lax.psum_scatter(
        contract_rows(selector, contrib), "inner", scatter_dimension=0, tiled=True
    )
    sep_whole = lax.all_gather(b_sep - t_sep, "inner", axis=0, tiled=True)
    y_sep = matmul_exact(sep_linv, sep_whole)
    t_root = lax.psum_scatter(
        matmul_exact(sep_lower, y_sep), ("outer", "inner"), scatter_dimension=0, tiled=True
    )
    root_rhs = lax.all_gather(b_root - t_root, ("outer", "inner"), axis=0, tiled=True)
    y_root = matmul_exact(root_linv, root_rhs)
    y_root_all = lax.all_gather(y_root, ("outer", "inner"), axis=0, tiled=True)
    x_root = matmul_exact(root_uinv, y_root_all)
    x_root_all = lax.all_gather(x_root, ("outer", "inner"), axis=0, tiled=True)
    z_sep = y_sep - matmul_exact(sep_upper, x_root_all)
    z_sep_all = lax.all_gather(z_sep, "inner", axis=0, tiled=True)
    x_sep = matmul_exact(sep_uinv, z_sep_all)
    x_sep_all = lax.all_gather(x_sep, "inner", axis=0, tiled=True)
    coupled = matmul_exact(selector, x_sep_all)
    x_leaf = matmul_exact(leaf_uinv, y_leaf - matmul_exact(leaf_upper, coupled))
    node_count = float(
        lax.axis_size("outer") * lax.axis_size("inner") * (b_leaf.shape[0] + sep_local + root_local)
    )
    pieces_x = (x_leaf, x_sep, x_root)
    pieces_q = (basis_leaf, basis_sep, basis_root)
    projected = (
        contract_rows(basis_leaf, x_leaf)
        + contract_rows(basis_sep, x_sep)
        + contract_rows(basis_root, x_root)
    )
    coefficients = lax.psum(projected, ("outer", "inner")) / node_count
    cleaned = [
        values - matmul_exact(basis, coefficients) for basis, values in zip(pieces_q, pieces_x)
    ]
    local_gram = (
        contract_rows(cleaned[0], cleaned[0])
        + contract_rows(cleaned[1], cleaned[1])
        + contract_rows(cleaned[2], cleaned[2])
    )
    gram_matrix = lax.psum(local_gram, ("outer", "inner")) / node_count
    chol_lower = jnp.linalg.cholesky(gram_matrix)
    inverse_lower = lax.linalg.triangular_solve(
        chol_lower, jnp.eye(ports, dtype=jnp.float32), left_side=True, lower=True
    )
    v_leaf = matmul_exact(cleaned[0], inverse_lower.T)
    v_sep = matmul_exact(cleaned[1], inverse_lower.T)
    v_root = matmul_exact(cleaned[2], inverse_lower.T)
    block_rows = block_cols.shape[0]
    stored = block_cols.shape[1]
    block_size = g_blocks.shape[1]
    blocked = v_leaf.reshape(block_rows, block_size, ports)
    picked = blocked[block_cols]
    g_tiles = g_blocks.reshape(block_rows, stored, block_size, block_size)
    c_tiles = c_blocks.reshape(block_rows, stored, block_size, block_size)
    g_image = jnp.einsum("rwij,rwjp->rip", g_tiles, picked, precision=lax.Precision.HIGHEST)
    c_image = jnp.einsum("rwij,rwjp->rip", c_tiles, picked, precision=lax.Precision.HIGHEST)
    g_local = jnp.einsum("rip,riq->pq", blocked, g_image, precision=lax.Precision.HIGHEST)
    c_local = jnp.einsum("rip,riq->pq", blocked, c_image, precision=lax.Precision.HIGHEST)
    g_summed, c_summed = lax.psum((g_local, c_local), ("outer", "inner"))
    return (v_leaf, v_sep, v_root, coefficients, g_summed / node_count, c_summed / node_count)


def solution(mesh):
    return jax.shard_map(
        shards,
        mesh=mesh,
        in_specs=(
            P(("outer", "inner"), None),
            P(("outer", "inner"), None),
            P(("outer", "inner"), None),
            P(("outer", "inner"), None),
            P(("outer", "inner"), None),
            P(("outer", "inner"), None),
            P(("outer", "inner"), None),
            P(("outer", "inner"), None),
            P(("outer", "inner"), None),
            P(("outer", "inner"), None),
            P(None, ("outer", "inner")),
            P(("outer", "inner"), None),
            P(("outer", "inner"), None),
            P(("outer", "inner"), None),
            P(("outer", "inner"), None),
            P(("outer", "inner"), None),
            P(("outer", "inner"), None),
            P(("outer", "inner"), None),
            P(("outer", "inner"), None),
            P(("outer", "inner"), None),
        ),
        out_specs=(
            P(("outer", "inner"), None),
            P(("outer", "inner"), None),
            P(("outer", "inner"), None),
            P(),
            P(),
            P(),
        ),
        check_vma=False,
    )
```

profile of v0, /device:TPU:1, one launch (start us, length us, event | category | flops | bytes accessed | tf_op | source)
XLA Modules:
  0.0 1057.3 jit_solution(8577901284034292284)
XLA Ops:
  7.2 1.4 fusion.16
  9.7 1.0 fusion.8
  12.7 112.8 %all-reduce.9.cloned.1.call-done = f32[256,64]{1,0:T(8,128)} async-done(((f32[256,64]{1,0:T(8,128)}), f32[256,64]{1,0:T(8,128)}) %all-reduce.9.cloned.1.call-update) | async-done | bytes 65552
  125.5 0.7 dynamic-slice_subtract_fusion.1
  126.2 25.7 %all_gather.18 = f32[256,64]{1,0:T(8,128)S(1)} all-gather(f32[8,64]{1,0:T(8,128)S(1)} %dynamic-slice_subtract_fusion.1), channel_id=1, replica_groups=mesh['outer'=8,'inner'=32] {'inner'}, dimensions={0}, use_global_device_ids=true | all-gather | bytes 67584 | tf_op jit(solution)/shard_map/all_gather | solution.py:55
  153.3 1.3 copy.47
  155.4 251.8 %all-reduce.11.cloned.1.call-done = f32[2048,64]{1,0:T(8,128)} async-done(((f32[2048,64]{1,0:T(8,128)}), f32[2048,64]{1,0:T(8,128)}) %all-reduce.11.cloned.1.call-update) | async-done | bytes 524304
  407.2 0.7 dynamic-slice_subtract_fusion
  407.9 63.2 %all_gather.19 = f32[2048,64]{1,0:T(8,128)S(1)} all-gather(f32[8,64]{1,0:T(8,128)S(1)} %dynamic-slice_subtract_fusion), channel_id=1, replica_groups=mesh['outer'=8,'inner'=32] {'outer','inner'}, dimensions={0}, use_global_device_ids=true | all-gather | bytes 526336 | tf_op jit(solution)/shard_map/all_gather | solution.py:60
  471.7 60.2 %all_gather.20 = f32[2048,64]{1,0:T(8,128)S(1)} all-gather(f32[8,64]{1,0:T(8,128)S(1)} %convolution_bitcast_fusion.8), channel_id=1, replica_groups=mesh['outer'=8,'inner'=32] {'outer','inner'}, dimensions={0}, use_global_device_ids=true | all-gather | bytes 526336 | tf_op jit(solution)/shard_map/all_gather | solution.py:62
  532.6 60.4 %all_gather.21 = f32[2048,64]{1,0:T(8,128)S(1)} all-gather(f32[8,64]{1,0:T(8,128)S(1)} %bitcast.121), channel_id=1, replica_groups=mesh['outer'=8,'inner'=32] {'outer','inner'}, dimensions={0}, use_global_device_ids=true | all-gather | bytes 526336 | tf_op jit(solution)/shard_map/all_gather | solution.py:64
  593.7 23.3 %all_gather.22 = f32[256,64]{1,0:T(8,128)S(1)} all-gather(f32[8,64]{1,0:T(8,128)S(1)} %fusion.5), channel_id=1, replica_groups=mesh['outer'=8,'inner'=32] {'inner'}, dimensions={0}, use_global_device_ids=true | all-gather | bytes 67584 | tf_op jit(solution)/shard_map/all_gather | solution.py:66
  617.2 23.0 %all_gather.23 = f32[256,64]{1,0:T(8,128)S(1)} all-gather(f32[8,64]{1,0:T(8,128)S(1)} %bitcast.122), channel_id=1, replica_groups=mesh['outer'=8,'inner'=32] {'inner'}, dimensions={0}, use_global_device_ids=true | all-gather | bytes 67584 | tf_op jit(solution)/shard_map/all_gather | solution.py:68
  642.0 1.1 fusion.1
  643.1 237.7 %all-reduce.7.cloned.1.call-done = f32[512,64]{0,1:T(8,128)} async-done(((f32[512,64]{0,1:T(8,128)}), f32[512,64]{0,1:T(8,128)}) %all-reduce.7.cloned.1.call-update) | async-done | bytes 131088 | tf_op jit(solution)/shard_map/psum | solution.py:81
  880.8 0.9 broadcast_multiply_fusion
  883.5 76.0 %psum.29 = f32[64,64]{0,1:T(8,128)S(1)} all-reduce(f32[64,64]{0,1:T(8,128)S(1)} %convolution_add_fusion.1), channel_id=1, replica_groups=mesh['outer'=8,'inner'=32] {'outer','inner'}, use_global_device_ids=true, to_apply=%region_3.0 | all-reduce | flops 4096 | bytes 32768 | tf_op jit(solution)/shard_map/psum | solution.py:90
  959.7 5.8 cholesky.17
  966.9 4.9 custom-call.6
  972.2 0.8 fusion.27
  973.0 0.8 fusion.26
  976.2 73.1 %all-reduce.2 = (f32[64,64]{0,1:T(8,128)S(1)}, f32[64,64]{0,1:T(8,128)S(1)}) all-reduce(f32[64,64]{0,1:T(8,128)S(1)} %convolution_bitcast_fusion.5, f32[64,64]{0,1:T(8,128)S(1)} %convolution_bitcast_fusion.4), channel_id=1, replica_groups=mesh['outer'=8,'inner'=32] {'outer','inner'}, use_global_device_ids=true, to_apply=%region_6.7 | all-reduce | flops 8192 | bytes 65536 | tf_op jit(solution)/shard_map/psum | solution.py:109
  1049.4 0.7 copy.57
  1050.1 0.7 copy.58
  (85 shorter events, 14.6 us)
Async XLA Ops:
  7.2 967.2 %copy-start = (f32[1024,128]{1,0:T(8,128)S(1)}, f32[1024,128]{1,0:T(8,128)}, u32[]{:S(2)}) copy-start(f32[1024,128]{1,0:T(8,128)} %param.38) | copy-start | bytes 1572868
  7.2 1.5 copy-start.6
  7.2 118.3 %all-reduce.9.cloned.1.call-start = ((), (), s32[]{:S(2)}) async-start(), calls=%async_computation.1 | async-start | bytes 262144
  9.0 0.7 copy-start.16
  10.8 396.5 %all-reduce.11.cloned.1.call-start = ((), (), s32[]{:S(2)}) async-start(), calls=%async_computation.2 | async-start | bytes 2097152
  10.8 0.7 copy-start.20
  11.5 114.0 %copy-start.17 = (f32[8,64]{1,0:T(8,128)S(1)}, f32[8,64]{1,0:T(8,128)}, u32[]{:S(2)}) copy-start(f32[8,64]{1,0:T(8,128)} %param.21) | copy-start | bytes 6148
  126.2 25.7 %copy-start.14 = (f32[8,256]{1,0:T(8,128)S(1)}, f32[8,256]{1,0:T(8,128)}, u32[]{:S(2)}) copy-start(f32[8,256]{1,0:T(8,128)} %param.28) | copy-start | bytes 24580
  151.8 0.8 copy-start.8
  154.7 0.7 copy-start.19
  154.7 252.5 %copy-start.18 = (f32[8,64]{1,0:T(8,128)S(1)}, f32[8,64]{1,0:T(8,128)}, u32[]{:S(2)}) copy-start(f32[8,64]{1,0:T(8,128)} %param.22) | copy-start | bytes 6148
  154.7 726.1 %all-reduce.7.cloned.1.call-start = ((), (), s32[]{:S(2)}) async-start(), calls=%async_computation | async-start | bytes 262144 | tf_op jit(solution)/shard_map/psum | solution.py:81
  407.9 63.2 %copy-start.9 = (f32[8,2048]{1,0:T(8,128)S(1)}, f32[8,2048]{1,0:T(8,128)}, u32[]{:S(2)}) copy-start(f32[8,2048]{1,0:T(8,128)} %param.32) | copy-start | bytes 196612
  471.7 60.2 %copy-start.10 = (f32[8,2048]{1,0:T(8,128)S(1)}, f32[8,2048]{1,0:T(8,128)}, u32[]{:S(2)}) copy-start(f32[8,2048]{1,0:T(8,128)} %param.33) | copy-start | bytes 196612
  532.6 60.4 %copy-start.11 = (f32[8,2048]{1,0:T(8,128)S(1)}, f32[8,2048]{1,0:T(8,128)}, u32[]{:S(2)}) copy-start(f32[8,2048]{1,0:T(8,128)} %param.31) | copy-start | bytes 196612
  593.7 23.3 %copy-start.15 = (f32[8,256]{1,0:T(8,128)S(1)}, f32[8,256]{1,0:T(8,128)}, u32[]{:S(2)}) copy-start(f32[8,256]{1,0:T(8,128)} %param.29) | copy-start | bytes 24580
  617.2 23.4 %copy-start.12 = (f32[8,512]{1,0:T(8,128)S(1)}, f32[8,512]{1,0:T(8,128)}, u32[]{:S(2)}) copy-start(f32[8,512]{1,0:T(8,128)} %param.35) | copy-start | bytes 49156
  640.2 0.7 copy-start.13
  640.2 1.0 copy-start.5
  640.6 1.1 copy-start.7
  640.9 1.1 copy-start.1
  881.8 0.8 copy-start.2
  972.2 3.8 copy-start.3
  974.3 1.0 copy-start.4
Sparse Core Ops, SparseCore 0:
  11.8 113.6 all-reduce.8
  154.8 252.3 all-reduce.10
  643.3 237.5 all-reduce.6
where the time goes:
time: 1060 us
  waiting for transfers between devices  602 us (57%)
  blocking collectives  405 us (38%)
  between operations  14.7 us (1%)
  other arithmetic  14.4 us (1%)
  matrix products  14 us (1%)
    unnamed x5, waiting for transfers between devices  365 us
    psum x1, waiting for transfers between devices, shards(): coefficients = lax.psum(projected, ('outer', 'inner')) / node_count  238 us
    psum x1, blocking collectives, shards(): gram_matrix = lax.psum(local_gram, ('outer', 'inner')) / node_count  76 us
    psum x1, blocking collectives, shards(): g_summed, c_summed = lax.psum((g_local, c_local), ('outer', 'inner'))  73.1 us
    all_gather x1, blocking collectives, shards(): lax.all_gather(b_root - t_root, ('outer', 'inner'), axis=0, tiled=True)  63.2 us
    all_gather x1, blocking collectives, shards(): x_root_all = lax.all_gather(x_root, ('outer', 'inner'), axis=0, tiled=True)  60.4 us
    all_gather x1, blocking collectives, shards(): y_root_all = lax.all_gather(y_root, ('outer', 'inner'), axis=0, tiled=True)  60.2 us
    all_gather x1, blocking collectives, shards(): sep_whole = lax.all_gather(b_sep - t_sep, 'inner', axis=0, tiled=True)  25.7 us
  transfers between devices with their start and end apart: 3, of which 3 were waited for; matrix products, arithmetic and copies ran while one was open for 0% of the time, Pallas kernels for 0%

commit v1 on v0

--- a/solution.py
+++ b/solution.py
@@ -2,6 +2,10 @@
 import jax.numpy as jnp
 from jax import lax
 from jax.sharding import PartitionSpec as P
+
+derive_things = lambda u, k_dim: jnp.concatenate(
+    lax.all_to_all(jnp.stack([u for _ in range(lax.axis_size("inner"))]), "inner", 0, 0), k_dim
+)
 
 
 def matmul_exact(left, right):
@@ -63,7 +67,7 @@
     x_root = matmul_exact(root_uinv, y_root_all)
     x_root_all = lax.all_gather(x_root, ("outer", "inner"), axis=0, tiled=True)
     z_sep = y_sep - matmul_exact(sep_upper, x_root_all)
-    z_sep_all = lax.all_gather(z_sep, "inner", axis=0, tiled=True)
+    z_sep_all = derive_things(z_sep, 0)
     x_sep = matmul_exact(sep_uinv, z_sep_all)
     x_sep_all = lax.all_gather(x_sep, "inner", axis=0, tiled=True)
     coupled = matmul_exact(selector, x_sep_all)

time: 1060 us -> 1050 us (level)
  blocking collectives: 405 us -> 382 us
    all_gather x1 -> x0, blocking collectives: 23.3 us -> none  [shards(): z_sep_all = lax.all_gather(z_sep, 'inner', axis=0, tiled=True)]
  transfers between devices with their start and end apart: 3 -> 4, of which waited for: 3 -> 4; matrix products, arithmetic and copies ran while one was open for 0% -> 0% of each run, Pallas kernels for 0% -> 0%
where the time goes in v1:
time: 1050 us
  waiting for transfers between devices  609 us (58%)
  blocking collectives  382 us (36%)
  other arithmetic  15.2 us (1%)
  between operations  14.8 us (1%)
  matrix products  14 us (1%)
    unnamed x5, waiting for transfers between devices  365 us
    psum x1, waiting for transfers between devices, shards(): coefficients = lax.psum(projected, ('outer', 'inner')) / node_count  238 us
    psum x1, blocking collectives, shards(): gram_matrix = lax.psum(local_gram, ('outer', 'inner')) / node_count  76 us
    psum x1, blocking collectives, shards(): g_summed, c_summed = lax.psum((g_local, c_local), ('outer', 'inner'))  73.1 us
    all_gather x1, blocking collectives, shards(): lax.all_gather(b_root - t_root, ('outer', 'inner'), axis=0, tiled=True)  63.1 us
    all_gather x1, blocking collectives, shards(): x_root_all = lax.all_gather(x_root, ('outer', 'inner'), axis=0, tiled=True)  60.4 us
    all_gather x1, blocking collectives, shards(): y_root_all = lax.all_gather(y_root, ('outer', 'inner'), axis=0, tiled=True)  60.2 us
    all_gather x1, blocking collectives, shards(): sep_whole = lax.all_gather(b_sep - t_sep, 'inner', axis=0, tiled=True)  25.7 us
  transfers between devices with their start and end apart: 4, of which 4 were waited for; matrix products, arithmetic and copies ran while one was open for 0% of the time, Pallas kernels for 0%

profile of v1, /device:TPU:1, one launch (start us, length us, event | category | flops | bytes accessed | tf_op | source)
XLA Modules:
  0.0 1048.3 jit_solution(3166842034302406417)
XLA Ops:
  7.2 1.4 fusion.18
  9.7 1.0 fusion.8
  12.7 112.8 %all-reduce.9.cloned.1.call-done = f32[256,64]{1,0:T(8,128)} async-done(((f32[256,64]{1,0:T(8,128)}), f32[256,64]{1,0:T(8,128)}) %all-reduce.9.cloned.1.call-update) | async-done | bytes 65552
  126.2 25.7 %all_gather.15 = f32[256,64]{1,0:T(8,128)S(1)} all-gather(f32[8,64]{1,0:T(8,128)S(1)} %dynamic-slice_subtract_fusion.1), channel_id=1, replica_groups=mesh['outer'=8,'inner'=32] {'inner'}, dimensions={0}, use_global_device_ids=true | all-gather | bytes 67584 | tf_op jit(solution)/shard_map/all_gather | solution.py:59
  153.3 1.4 copy.47
  155.5 251.8 %all-reduce.11.cloned.1.call-done = f32[2048,64]{1,0:T(8,128)} async-done(((f32[2048,64]{1,0:T(8,128)}), f32[2048,64]{1,0:T(8,128)}) %all-reduce.11.cloned.1.call-update) | async-done | bytes 524304
  407.9 63.1 %all_gather.16 = f32[2048,64]{1,0:T(8,128)S(1)} all-gather(f32[8,64]{1,0:T(8,128)S(1)} %dynamic-slice_subtract_fusion), channel_id=1, replica_groups=mesh['outer'=8,'inner'=32] {'outer','inner'}, dimensions={0}, use_global_device_ids=true | all-gather | bytes 526336 | tf_op jit(solution)/shard_map/all_gather | solution.py:64
  471.7 60.2 %all_gather.17 = f32[2048,64]{1,0:T(8,128)S(1)} all-gather(f32[8,64]{1,0:T(8,128)S(1)} %convolution_bitcast_fusion.8), channel_id=1, replica_groups=mesh['outer'=8,'inner'=32] {'outer','inner'}, dimensions={0}, use_global_device_ids=true | all-gather | bytes 526336 | tf_op jit(solution)/shard_map/all_gather | solution.py:66
  532.6 60.4 %all_gather.18 = f32[2048,64]{1,0:T(8,128)S(1)} all-gather(f32[8,64]{1,0:T(8,128)S(1)} %bitcast.123), channel_id=1, replica_groups=mesh['outer'=8,'inner'=32] {'outer','inner'}, dimensions={0}, use_global_device_ids=true | all-gather | bytes 526336 | tf_op jit(solution)/shard_map/all_gather | solution.py:68
  593.7 0.8 reshape.55
  594.5 4.4 all-to-all-start
  599.2 7.0 all-to-all-done
  606.7 0.8 reduce.6
  608.4 23.1 %all_gather.19 = f32[256,64]{1,0:T(8,128)S(1)} all-gather(f32[8,64]{1,0:T(8,128)S(1)} %bitcast.124), channel_id=1, replica_groups=mesh['outer'=8,'inner'=32] {'inner'}, dimensions={0}, use_global_device_ids=true | all-gather | bytes 67584 | tf_op jit(solution)/shard_map/all_gather | solution.py:72
  633.0 1.1 fusion.1
  634.1 237.7 %all-reduce.7.cloned.1.call-done = f32[512,64]{0,1:T(8,128)} async-done(((f32[512,64]{0,1:T(8,128)}), f32[512,64]{0,1:T(8,128)}) %all-reduce.7.cloned.1.call-update) | async-done | bytes 131088 | tf_op jit(solution)/shard_map/psum | solution.py:85
  871.9 0.9 broadcast_multiply_fusion
  874.6 76.0 %psum.29 = f32[64,64]{0,1:T(8,128)S(1)} all-reduce(f32[64,64]{0,1:T(8,128)S(1)} %convolution_add_fusion.1), channel_id=1, replica_groups=mesh['outer'=8,'inner'=32] {'outer','inner'}, use_global_device_ids=true, to_apply=%region_3.0 | all-reduce | flops 4096 | bytes 32768 | tf_op jit(solution)/shard_map/psum | solution.py:94
  950.7 5.8 cholesky.17
  957.9 4.9 custom-call.6
  963.2 0.8 fusion.28
  964.0 0.8 fusion.27
  967.3 73.1 %all-reduce.2 = (f32[64,64]{0,1:T(8,128)S(1)}, f32[64,64]{0,1:T(8,128)S(1)}) all-reduce(f32[64,64]{0,1:T(8,128)S(1)} %convolution_bitcast_fusion.5, f32[64,64]{0,1:T(8,128)S(1)} %convolution_bitcast_fusion.4), channel_id=1, replica_groups=mesh['outer'=8,'inner'=32] {'outer','inner'}, use_global_device_ids=true, to_apply=%region_6.7 | all-reduce | flops 8192 | bytes 65536 | tf_op jit(solution)/shard_map/psum | solution.py:113
  1040.4 0.7 copy.57
  (91 shorter events, 17.9 us)
Async XLA Ops:
  7.2 958.2 %copy-start = (f32[1024,128]{1,0:T(8,128)S(1)}, f32[1024,128]{1,0:T(8,128)}, u32[]{:S(2)}) copy-start(f32[1024,128]{1,0:T(8,128)} %param.38) | copy-start | bytes 1572868
  7.2 1.5 copy-start.6
  7.2 118.3 %all-reduce.9.cloned.1.call-start = ((), (), s32[]{:S(2)}) async-start(), calls=%async_computation.2 | async-start | bytes 262144
  9.0 0.7 copy-start.16
  10.8 396.4 %all-reduce.11.cloned.1.call-start = ((), (), s32[]{:S(2)}) async-start(), calls=%async_computation.3 | async-start | bytes 2097152
  10.8 0.7 copy-start.20
  11.5 114.0 %copy-start.17 = (f32[8,64]{1,0:T(8,128)S(1)}, f32[8,64]{1,0:T(8,128)}, u32[]{:S(2)}) copy-start(f32[8,64]{1,0:T(8,128)} %param.21) | copy-start | bytes 6148
  126.2 25.7 %copy-start.14 = (f32[8,256]{1,0:T(8,128)S(1)}, f32[8,256]{1,0:T(8,128)}, u32[]{:S(2)}) copy-start(f32[8,256]{1,0:T(8,128)} %param.28) | copy-start | bytes 24580
  151.8 0.8 copy-start.8
  154.7 252.5 %copy-start.18 = (f32[8,64]{1,0:T(8,128)S(1)}, f32[8,64]{1,0:T(8,128)}, u32[]{:S(2)}) copy-start(f32[8,64]{1,0:T(8,128)} %param.22) | copy-start | bytes 6148
  407.9 63.2 %copy-start.9 = (f32[8,2048]{1,0:T(8,128)S(1)}, f32[8,2048]{1,0:T(8,128)}, u32[]{:S(2)}) copy-start(f32[8,2048]{1,0:T(8,128)} %param.32) | copy-start | bytes 196612
  471.7 60.2 %copy-start.10 = (f32[8,2048]{1,0:T(8,128)S(1)}, f32[8,2048]{1,0:T(8,128)}, u32[]{:S(2)}) copy-start(f32[8,2048]{1,0:T(8,128)} %param.33) | copy-start | bytes 196612
  532.6 60.4 %copy-start.11 = (f32[8,2048]{1,0:T(8,128)S(1)}, f32[8,2048]{1,0:T(8,128)}, u32[]{:S(2)}) copy-start(f32[8,2048]{1,0:T(8,128)} %param.31) | copy-start | bytes 196612
  594.5 4.4 copy-start.13
  594.5 11.7 %all-to-all-start = ((f32[32,1,512]{2,1,0:T(1,128)}), f32[32,1,512]{2,1,0:T(1,128)S(1)}, u32[]{:S(2)}, u32[]{:S(2)}) async-start(f32[32,1,512]{2,1,0:T(1,128)} %reshape.55), calls=%async_computation | async-start | bytes 131072 | tf_op jit(solution)/shard_map/all_to_all | solution.py:7
  598.9 273.0 %all-reduce.7.cloned.1.call-start = ((), (), s32[]{:S(2)}) async-start(), calls=%async_computation.1 | async-start | bytes 262144 | tf_op jit(solution)/shard_map/psum | solution.py:85
  607.6 0.7 copy-start.15
  608.4 23.8 %copy-start.5 = (f32[256,256]{1,0:T(8,128)S(1)}, f32[256,256]{1,0:T(8,128)}, u32[]{:S(2)}) copy-start(f32[256,256]{1,0:T(8,128)} %param.26) | copy-start | bytes 786436
  608.4 23.4 %copy-start.12 = (f32[8,512]{1,0:T(8,128)S(1)}, f32[8,512]{1,0:T(8,128)}, u32[]{:S(2)}) copy-start(f32[8,512]{1,0:T(8,128)} %param.35) | copy-start | bytes 49156
  631.5 1.1 copy-start.7
  631.9 1.1 copy-start.1
  872.8 0.8 copy-start.2
  963.2 3.8 copy-start.3
  965.3 1.0 copy-start.4
  (1 other events, 0.7 us)
Sparse Core Ops, SparseCore 0:
  11.8 113.6 all-reduce.8
  154.8 252.3 all-reduce.10
  634.2 237.5 all-reduce.6
